TPU v7x, 32 devices: a whole 2x2x4 slice. The times are simulated.
32 devices in a mesh: row: 8 (over z, y), col: 4 (over x, core).
Axes of the slice: x: 2, y: 2, z: 4, core: 2. Of those that a mesh axis runs over, the one named last changes fastest.
Arguments:
- queries: bfloat16 [4096, 768], P(('row', 'col')), may hold values from -6 to 6
- key_rows: bfloat16 [4096, 768], P(('col', 'row')), may hold values from -6 to 6
- values: bfloat16 [4096, 768], P(('col', 'row')), may hold values from -6 to 6
- out_grad: bfloat16 [4096, 768], P(('row', 'col')), may hold values from -6 to 6
- block_pairs: int32 [32, 32, 2], P(('row', 'col')), may hold values from 0 to 7, as said below
- pair_count: int32 [32], P(('row', 'col')), may hold values from 1 to 32, as said below
- edge_mask: int32 [32, 32, 128, 128], P(('row', 'col')), may hold values from 0 to 1, as said below
Outputs:
- attention_out: bfloat16 [4096, 768], P(('row', 'col'))
- query_grad: float32 [4096, 768], P(('row', 'col'))
- key_grad: float32 [4096, 768], P(('col', 'row'))
- value_grad: float32 [4096, 768], P(('col', 'row'))
Inputs may be any that keep to these rules, and one draw needn't show every extreme that they name: `block_pairs`: the slots of one device name distinct block pairs of its tile, the first coordinate below 4, the second below 8. Every block pair of a target block with the source block of the same global number stands among the live slots of its device. `pair_count`: some device has all 32 slots live. `edge_mask`: in every live block pair of a target block with the source block of the same number, each node has an edge to itself and to the node whose index differs in the lowest bit.
All inputs are finite; a program needn't handle non-finite values.
Results may differ from a plain program's by a relative error of at most 0.015.
Values may be sent and summed in bfloat16 or wider, within the bound.
A program may use at most 192 MiB of HBM per device.

v0:
```python
import functools

import jax
import jax.numpy as jnp
from jax import lax
from jax.experimental import pallas as pl
from jax.experimental.pallas import tpu as pltpu
from jax.sharding import PartitionSpec as P

HEADS = 8
HEAD_DIM = 96
BLOCK = 128


NEGATIVE = -1e30


def on_device(queries, key_rows, values, out_grad, block_pairs, pair_count, edge_mask):
    score_scale = HEAD_DIM ** (-0.5)
    targets, cotangent = (
        lax.all_gather(queries, "col", axis=0, tiled=True),
        lax.all_gather(out_grad, "col", axis=0, tiled=True),
    )
    sources, source_values = (
        lax.all_gather(key_rows, "row", axis=0, tiled=True),
        lax.all_gather(values, "row", axis=0, tiled=True),
    )
    own_rows = queries.shape[0]
    target_rows = targets.shape[0]
    source_rows = sources.shape[0]
    target_blocks = target_rows // BLOCK
    source_blocks = source_rows // BLOCK
    query_blocks = targets.reshape(target_blocks, BLOCK, HEADS, HEAD_DIM)
    grad_blocks = cotangent.reshape(target_blocks, BLOCK, HEADS, HEAD_DIM)
    key_blocks = sources.reshape(source_blocks, BLOCK, HEADS, HEAD_DIM)
    value_blocks = source_values.reshape(source_blocks, BLOCK, HEADS, HEAD_DIM)
    slot_total = edge_mask.shape[1]
    group_size = min(8, slot_total)
    turn_count = slot_total // group_size
    pair_list = block_pairs[0]
    live_slots = jnp.arange(slot_total, dtype=jnp.int32) < pair_count[0]
    keep_all = (edge_mask[0] > 0) & live_slots[:, None, None]

    def group_scores(turn_index):
        first_slot = turn_index * group_size
        target_ids = lax.dynamic_slice_in_dim(pair_list[:, 0], first_slot, group_size)
        source_ids = lax.dynamic_slice_in_dim(pair_list[:, 1], first_slot, group_size)
        keep_mask = lax.dynamic_slice_in_dim(keep_all, first_slot, group_size, 0)[:, None, :, :]
        scores = (
            jnp.einsum(
                "gihd,gjhd->ghij",
                query_blocks[target_ids],
                key_blocks[source_ids],
                preferred_element_type=jnp.float32,
            )
            * score_scale
        )
        return (target_ids, source_ids, keep_mask, scores)

    def max_turn(turn_index, running_max):
        target_ids, source_ids, keep_mask, scores = group_scores(turn_index)
        row_top = jnp.max(jnp.where(keep_mask, scores, NEGATIVE), axis=3)
        return running_max.at[target_ids].max(row_top)

    local_max = lax.fori_loop(
        0, turn_count, max_turn, jnp.full((target_blocks, HEADS, BLOCK), NEGATIVE, jnp.float32)
    )
    row_max = lax.pmax(local_max, "col")

    def sum_turn(turn_index, carry):
        numer_sum, weight_sum = carry
        target_ids, source_ids, keep_mask, scores = group_scores(turn_index)
        weights = jnp.exp(jnp.where(keep_mask, scores - row_max[target_ids][..., None], NEGATIVE))
        rounded = weights.astype(jnp.bfloat16)
        mixed = jnp.einsum(
            "ghij,gjhd->gihd", rounded, value_blocks[source_ids], preferred_element_type=jnp.float32
        )
        numer_sum = numer_sum.at[target_ids].add(mixed.reshape(group_size, BLOCK, HEADS * HEAD_DIM))
        weight_sum = weight_sum.at[target_ids].add(jnp.sum(weights, axis=3))
        return (numer_sum, weight_sum)

    numer_init = jnp.zeros((target_blocks, BLOCK, HEADS * HEAD_DIM), jnp.float32)
    total_init = jnp.zeros((target_blocks, HEADS, BLOCK), jnp.float32)
    numer_sum, weight_sum = lax.fori_loop(0, turn_count, sum_turn, (numer_init, total_init))
    numer_flat = numer_sum.reshape(target_rows, HEADS * HEAD_DIM)
    numer_all, total_all = lax.psum((numer_flat, weight_sum), "col")
    heads_out = (
        numer_all.reshape(target_blocks, BLOCK, HEADS, HEAD_DIM)
        / jnp.transpose(total_all, (0, 2, 1))[..., None]
    )
    out_all = heads_out.astype(jnp.bfloat16).reshape(target_rows, HEADS * HEAD_DIM)
    attention_out = lax.dynamic_slice_in_dim(out_all, lax.axis_index("col") * own_rows, own_rows, 0)
    products = (cotangent.astype(jnp.float32) * out_all.astype(jnp.float32)).reshape(
        target_blocks, BLOCK, HEADS, HEAD_DIM
    )
    row_delta = jnp.transpose(jnp.sum(products, axis=3), (0, 2, 1))

    def back_turn(turn_index, carry):
        query_acc, key_acc, value_acc = carry
        target_ids, source_ids, keep_mask, scores = group_scores(turn_index)
        probs = (
            jnp.exp(jnp.where(keep_mask, scores - row_max[target_ids][..., None], NEGATIVE))
            / total_all[target_ids][..., None]
        )
        grad_group = grad_blocks[target_ids]
        grad_dots = jnp.einsum(
            "gihd,gjhd->ghij",
            grad_group,
            value_blocks[source_ids],
            preferred_element_type=jnp.float32,
        )
        score_grads = (probs * (grad_dots - row_delta[target_ids][..., None]) * score_scale).astype(
            jnp.bfloat16
        )
        probs_rounded = probs.astype(jnp.bfloat16)
        query_part = jnp.einsum(
            "ghij,gjhd->gihd",
            score_grads,
            key_blocks[source_ids],
            preferred_element_type=jnp.float32,
        )
        key_part = jnp.einsum(
            "ghij,gihd->gjhd",
            score_grads,
            query_blocks[target_ids],
            preferred_element_type=jnp.float32,
        )
        value_part = jnp.einsum(
            "ghij,gihd->gjhd", probs_rounded, grad_group, preferred_element_type=jnp.float32
        )
        query_acc = query_acc.at[target_ids].add(
            query_part.reshape(group_size, BLOCK, HEADS * HEAD_DIM)
        )
        key_acc = key_acc.at[source_ids].add(key_part.reshape(group_size, BLOCK, HEADS * HEAD_DIM))
        value_acc = value_acc.at[source_ids].add(
            value_part.reshape(group_size, BLOCK, HEADS * HEAD_DIM)
        )
        return (query_acc, key_acc, value_acc)

    query_init = jnp.zeros((target_blocks, BLOCK, HEADS * HEAD_DIM), jnp.float32)
    source_init = jnp.zeros((source_blocks, BLOCK, HEADS * HEAD_DIM), jnp.float32)
    query_acc, key_acc, value_acc = lax.fori_loop(
        0, turn_count, back_turn, (query_init, source_init, source_init)
    )
    query_grad = lax.psum_scatter(
        query_acc.reshape(target_rows, HEADS * HEAD_DIM), "col", scatter_dimension=0, tiled=True
    )
    key_grad, value_grad = (
        lax.psum_scatter(
            key_acc.reshape(source_rows, HEADS * HEAD_DIM), "row", scatter_dimension=0, tiled=True
        ),
        lax.psum_scatter(
            value_acc.reshape(source_rows, HEADS * HEAD_DIM), "row", scatter_dimension=0, tiled=True
        ),
    )
    return (attention_out, query_grad, key_grad, value_grad)


MASKED = -1e30
FLOOR = -1e28
MESH = pl.DeviceIdType.MESH


def contract(left, right, left_dim, right_dim):
    return lax.dot_general(
        left,
        right,
        (((left_dim,), (right_dim,)), ((), ())),
        preferred_element_type=jnp.float32,
    )


def prepare_kernel(pair_ref, count_ref, q_ref, k_ref, v_ref, g_ref, mask_ref, qg_ref, kv_ref, bias_ref):
    for src, dst, first in ((q_ref, qg_ref, 0), (g_ref, qg_ref, HEADS), (k_ref, kv_ref, 0), (v_ref, kv_ref, HEADS)):
        turned = jnp.transpose(src[...].astype(jnp.float32)).astype(jnp.bfloat16)
        dst[first : first + HEADS] = turned.reshape(HEADS, HEAD_DIM, BLOCK)
    bias_ref[...] = jnp.full(bias_ref.shape, MASKED, jnp.float32)

    @pl.loop(0, count_ref[0])
    def _(slot):
        target = pair_ref[slot, 0]
        source = pair_ref[slot, 1]
        kept = jnp.transpose(mask_ref[slot].astype(jnp.float32))
        bias_ref[source, target] = jnp.where(kept > 0.5, 0.0, MASKED)


def layer_kernel(
    n_ring,
    qg_own,
    kv_own,
    bias_ref,
    att_ref,
    qgrad_ref,
    kgrad_ref,
    vgrad_ref,
    kv_buf,
    qg_buf,
    weight_buf,
    dots_buf,
    chunk_stats,
    stat_buf,
    factor_buf,
    delta_buf,
    acc_buf,
    part_buf,
    right_out,
    right_in,
    left_out,
    left_in,
    core_out,
    core_in,
    chip_out,
    chip_in,
    ring_send,
    ring_recv,
    qg_send,
    qg_recv,
    stat_send,
    stat_recv,
    sum_send,
    sum_recv,
    col_send,
    col_recv,
    own_sem,
):
    scale = HEAD_DIM ** (-0.5)
    row = lax.axis_index("row")
    col = lax.axis_index("col")
    half_ring = n_ring // 2
    depth, side = row // 2, row % 2
    place = jnp.where(side == 0, depth, n_ring - 1 - depth)

    def row_at(position):
        wrapped = lax.rem(position + 2 * n_ring, n_ring)
        return jnp.where(wrapped < half_ring, 2 * wrapped, 2 * (n_ring - 1 - wrapped) + 1)

    right = (row_at(place + 1), col)
    left = (row_at(place - 1), col)
    core_col = col + 1 - 2 * (col % 2)
    chip_col = (col + 2) % 4
    core_peer = (row, core_col)
    chip_peer = (row, chip_col)
    others = [(row, (col + k) % 4) for k in range(1, 4)]
    pending = []

    def send(src, dst, send_sem, recv_sem, device):
        copy = pltpu.make_async_remote_copy(
            src_ref=src,
            dst_ref=dst,
            send_sem=send_sem,
            recv_sem=recv_sem,
            device_id=device,
            device_id_type=MESH,
        )
        copy.start()
        pending.append(copy)
        return copy

    barrier = pltpu.get_barrier_semaphore()
    for device in [right, left] + others:
        pl.semaphore_signal(barrier, inc=1, device_id=device, device_id_type=MESH)
    pl.semaphore_wait(barrier, 5)

    def lanes(index):
        return pl.ds(pl.multiple_of(index * BLOCK, BLOCK), BLOCK)

    def ring_right(step):
        part = pl.ds(0, 2 * HEADS if step < half_ring else HEADS)
        src = kv_own if step == 1 else kv_buf.at[step - 1]
        return send(
            src.at[part], kv_buf.at[step, part], ring_send.at[step], ring_recv.at[step], right
        )

    def ring_left(step):
        part = pl.ds(0, 2 * HEADS) if step < half_ring else pl.ds(HEADS, HEADS)
        src = kv_own if step == 1 else kv_buf.at[n_ring - step + 1]
        return send(
            src.at[part],
            kv_buf.at[n_ring - step, part],
            ring_send.at[half_ring + step],
            ring_recv.at[half_ring + step],
            left,
        )

    from_chip = send(qg_own, qg_buf.at[:, :, lanes(col)], qg_send.at[0], qg_recv.at[0], chip_peer)
    from_core = send(qg_own, qg_buf.at[:, :, lanes(col)], qg_send.at[1], qg_recv.at[1], core_peer)
    on_right = ring_right(1)
    on_left = ring_left(1)
    own_copy = pltpu.make_async_copy(qg_own, qg_buf.at[:, :, lanes(col)], own_sem.at[0])
    own_copy.start()
    kv_buf[0] = kv_own[...]
    own_copy.wait()
    from_chip.wait_recv()
    passed = send(
        qg_buf.at[:, :, lanes(chip_col)],
        qg_buf.at[:, :, lanes(chip_col)],
        qg_send.at[2],
        qg_recv.at[2],
        core_peer,
    )
    from_core.wait_recv()
    passed.wait_recv()

    width = 2 * BLOCK
    parts = qg_buf.shape[2] // width

    def stats_of(slot):
        source = row_at(place - slot)

        @pl.loop(0, HEADS)
        def _(head):
            key_t = kv_buf[slot, head]
            value_t = kv_buf[slot, HEADS + head]
            for part in range(parts):
                cut = pl.ds(part * width, width)
                bias = jnp.concatenate(
                    [bias_ref[source, 2 * part], bias_ref[source, 2 * part + 1]], axis=1
                )
                scores = contract(key_t, qg_buf[head, :, cut], 0, 0) * scale + bias
                dots = contract(value_t, qg_buf[HEADS + head, :, cut], 0, 0)
                top = jnp.maximum(jnp.max(scores, axis=0, keepdims=True), FLOOR)
                weights = jnp.exp(scores - top)
                weight_buf[slot, head, :, cut] = weights
                dots_buf[slot, head, :, cut] = dots
                chunk_stats[slot, head, 0:1, cut] = top
                chunk_stats[slot, head, 1:2, cut] = jnp.sum(weights, axis=0, keepdims=True)
                chunk_stats[slot, head, 2:3, cut] = jnp.sum(weights * dots, axis=0, keepdims=True)

    stats_of(0)
    for step in range(1, half_ring + 1):
        on_right.wait_recv()
        last_right = on_right
        if step < half_ring:
            on_right = ring_right(step + 1)
        on_left.wait_recv()
        if step < half_ring:
            on_left = ring_left(step + 1)
            stats_of(step)
            stats_of(n_ring - step)
        else:
            stats_of(step)

    @pl.loop(0, HEADS)
    def _(head):
        top = chunk_stats[0, head, 0:1]
        for slot in range(1, n_ring):
            top = jnp.maximum(top, chunk_stats[slot, head, 0:1])
        total = jnp.zeros_like(top)
        mixed = jnp.zeros_like(top)
        for slot in range(n_ring):
            factor = jnp.exp(chunk_stats[slot, head, 0:1] - top)
            total = total + factor * chunk_stats[slot, head, 1:2]
            mixed = mixed + factor * chunk_stats[slot, head, 2:3]
        stat_buf[0, head, 0:1] = top
        stat_buf[0, head, 1:2] = total
        stat_buf[0, head, 2:3] = mixed

    shared = [
        send(stat_buf.at[0], stat_buf.at[k], stat_send.at[k], stat_recv.at[k], others[k - 1])
        for k in range(1, 4)
    ]
    acc_buf[...] = jnp.zeros(acc_buf.shape, jnp.float32)
    for copy in shared:
        copy.wait_recv()

    @pl.loop(0, HEADS)
    def _(head):
        top = stat_buf[0, head, 0:1]
        for k in range(1, 4):
            top = jnp.maximum(top, stat_buf[k, head, 0:1])
        total = jnp.zeros_like(top)
        mixed = jnp.zeros_like(top)
        for k in range(4):
            factor = jnp.exp(stat_buf[k, head, 0:1] - top)
            total = total + factor * stat_buf[k, head, 1:2]
            mixed = mixed + factor * stat_buf[k, head, 2:3]
        inverse = 1.0 / total
        delta_buf[head, 0:1] = mixed * inverse
        for slot in range(n_ring):
            factor_buf[head, slot : slot + 1] = (
                jnp.exp(chunk_stats[slot, head, 0:1] - top) * inverse
            )

    def grads_of(slot):
        @pl.loop(0, HEADS)
        def _(head):
            key_t = kv_buf[slot, head]
            value_t = kv_buf[slot, HEADS + head]
            key_part = jnp.zeros((HEAD_DIM, BLOCK), jnp.float32)
            value_part = jnp.zeros((HEAD_DIM, BLOCK), jnp.float32)
            for part in range(parts):
                cut = pl.ds(part * width, width)
                probs = weight_buf[slot, head, :, cut] * factor_buf[head, slot : slot + 1, cut]
                score_grads = (
                    probs * (dots_buf[slot, head, :, cut] - delta_buf[head, 0:1, cut]) * scale
                ).astype(jnp.bfloat16)
                probs = probs.astype(jnp.bfloat16)
                key_part += contract(qg_buf[head, :, cut], score_grads, 1, 1)
                value_part += contract(qg_buf[HEADS + head, :, cut], probs, 1, 1)
                acc_buf[head, :, cut] += contract(key_t, score_grads, 1, 0)
                acc_buf[HEADS + head, :, cut] += contract(value_t, probs, 1, 0)
            part_buf[head] = key_part
            part_buf[HEADS + head] = value_part

    def pass_on(outgoing, incoming, hop, sems, device, arrived, first, count):
        if arrived is not None:
            arrived.wait_recv()

        @pl.loop(first, first + count)
        def _(index):
            term = part_buf[index]
            if arrived is not None:
                if hop == 1:
                    known = index < HEADS if sems == 0 else index >= HEADS
                    before = incoming[0, index].astype(jnp.float32)
                    term = term + jnp.where(known, before, 0.0)
                else:
                    term = term + incoming[hop - 1, index].astype(jnp.float32)
            outgoing[hop, index] = term.astype(jnp.bfloat16)

        at = pl.ds(first, count)
        return send(
            outgoing.at[hop, at],
            incoming.at[hop, at],
            sum_send.at[sems * half_ring + hop],
            sum_recv.at[sems * half_ring + hop],
            device,
        )

    def clear(ref, first):
        ref[0, pl.ds(first, HEADS)] = jnp.zeros((HEADS, HEAD_DIM, BLOCK), jnp.bfloat16)

    clear(right_in, HEADS)
    clear(left_in, 0)
    grads_of(half_ring)
    to_right = pass_on(right_out, right_in, 0, 0, right, None, 0, HEADS)
    to_left = pass_on(left_out, left_in, 0, 1, left, None, HEADS, HEADS)
    for hop in range(1, half_ring):
        grads_of(half_ring + hop)
        to_right = pass_on(right_out, right_in, hop, 0, right, to_right, 0, 2 * HEADS)
        grads_of(half_ring - hop)
        to_left = pass_on(left_out, left_in, hop, 1, left, to_left, 0, 2 * HEADS)
    grads_of(0)

    @pl.loop(0, 2 * HEADS)
    def _(index):
        core_out[0, index] = acc_buf[index, :, lanes(core_col)].astype(jnp.bfloat16)
        core_out[1, index] = acc_buf[index, :, lanes((core_col + 2) % 4)].astype(jnp.bfloat16)

    far = send(core_out.at[1], core_in.at[1], col_send.at[1], col_recv.at[1], core_peer)
    near = send(core_out.at[0], core_in.at[0], col_send.at[0], col_recv.at[0], core_peer)
    far.wait_recv()

    @pl.loop(0, 2 * HEADS)
    def _(index):
        chip_out[index] = (
            acc_buf[index, :, lanes(chip_col)] + core_in[1, index].astype(jnp.float32)
        ).astype(jnp.bfloat16)

    across = send(chip_out, chip_in, col_send.at[2], col_recv.at[2], chip_peer)
    near.wait_recv()
    to_right.wait_recv()
    to_left.wait_recv()

    @pl.loop(0, HEADS)
    def _(head):
        for first, ref in ((0, kgrad_ref), (HEADS, vgrad_ref)):
            index = head + first
            ref[head] = (
                part_buf[index]
                + right_in[half_ring - 1, index].astype(jnp.float32)
                + left_in[half_ring - 1, index].astype(jnp.float32)
            )

    across.wait_recv()

    @pl.loop(0, HEADS)
    def _(head):
        def summed(index):
            return (
                acc_buf[index, :, lanes(col)]
                + core_in[0, index].astype(jnp.float32)
                + chip_in[index].astype(jnp.float32)
            )

        qgrad_ref[head] = summed(head)
        att_ref[head] = summed(HEADS + head).astype(jnp.bfloat16)

    for copy in pending:
        copy.wait_send()


def fused(n_ring, n_col, queries, key_rows, values, out_grad, block_pairs, pair_count, edge_mask):
    vmem = pl.BlockSpec(memory_space=pltpu.VMEM)
    smem = pl.BlockSpec(memory_space=pltpu.SMEM)
    block = (2 * HEADS, HEAD_DIM, BLOCK)
    wide = n_col * BLOCK
    flat = (HEADS, HEAD_DIM, BLOCK)
    qg_own, kv_own, bias = pl.pallas_call(
        prepare_kernel,
        out_shape=(
            jax.ShapeDtypeStruct(block, jnp.bfloat16),
            jax.ShapeDtypeStruct(block, jnp.bfloat16),
            jax.ShapeDtypeStruct((n_ring, n_col, BLOCK, BLOCK), jnp.float32),
        ),
        in_specs=[smem] * 2 + [vmem] * 5,
        out_specs=(vmem, vmem, vmem),
        compiler_params=pltpu.CompilerParams(vmem_limit_bytes=24 * 2**20),
    )(block_pairs[0], pair_count, queries, key_rows, values, out_grad, edge_mask[0])
    half = n_ring // 2
    dma = pltpu.SemaphoreType.DMA
    outs = pl.pallas_call(
        functools.partial(layer_kernel, n_ring),
        out_shape=(
            jax.ShapeDtypeStruct(flat, jnp.bfloat16),
            jax.ShapeDtypeStruct(flat, jnp.float32),
            jax.ShapeDtypeStruct(flat, jnp.float32),
            jax.ShapeDtypeStruct(flat, jnp.float32),
        ),
        in_specs=[vmem] * 3,
        out_specs=(vmem,) * 4,
        scratch_shapes=[
            pltpu.VMEM((n_ring,) + block, jnp.bfloat16),
            pltpu.VMEM((2 * HEADS, HEAD_DIM, wide), jnp.bfloat16),
            pltpu.VMEM((n_ring, HEADS, BLOCK, wide), jnp.float32),
            pltpu.VMEM((n_ring, HEADS, BLOCK, wide), jnp.float32),
            pltpu.VMEM((n_ring, HEADS, 8, wide), jnp.float32),
            pltpu.VMEM((4, HEADS, 8, wide), jnp.float32),
            pltpu.VMEM((HEADS, n_ring, wide), jnp.float32),
            pltpu.VMEM((HEADS, 8, wide), jnp.float32),
            pltpu.VMEM((2 * HEADS, HEAD_DIM, wide), jnp.float32),
            pltpu.VMEM(block, jnp.float32),
            pltpu.VMEM((half,) + block, jnp.bfloat16),
            pltpu.VMEM((half,) + block, jnp.bfloat16),
            pltpu.VMEM((half,) + block, jnp.bfloat16),
            pltpu.VMEM((half,) + block, jnp.bfloat16),
            pltpu.VMEM((2,) + block, jnp.bfloat16),
            pltpu.VMEM((2,) + block, jnp.bfloat16),
            pltpu.VMEM(block, jnp.bfloat16),
            pltpu.VMEM(block, jnp.bfloat16),
            dma((2 * half + 1,)),
            dma((2 * half + 1,)),
            dma((3,)),
            dma((3,)),
            dma((4,)),
            dma((4,)),
            dma((2 * half,)),
            dma((2 * half,)),
            dma((3,)),
            dma((3,)),
            dma((1,)),
        ],
        compiler_params=pltpu.CompilerParams(
            collective_id=0, has_side_effects=True, vmem_limit_bytes=60 * 2**20
        ),
    )(qg_own, kv_own, bias)
    return tuple(jnp.transpose(out.reshape(HEADS * HEAD_DIM, BLOCK)) for out in outs)


def solution(mesh):
    n_row, n_col = mesh.shape["row"], mesh.shape["col"]
    placed = (
        P(("row", "col"), None),
        P(("col", "row"), None),
        P(("col", "row"), None),
        P(("row", "col"), None),
        P(("row", "col"), None, None),
        P(("row", "col")),
        P(("row", "col"), None, None, None),
    )

    def layer(queries, key_rows, values, out_grad, block_pairs, pair_count, edge_mask):
        args = (queries, key_rows, values, out_grad, block_pairs, pair_count, edge_mask)
        one_block = queries.shape[0] == BLOCK and key_rows.shape[0] == BLOCK
        full_tile = edge_mask.shape[1] == n_row * n_col
        if one_block and full_tile and n_row == 8 and n_col == 4:
            return fused(n_row, n_col, *args)
        return on_device(*args)

    return jax.shard_map(
        layer,
        mesh=mesh,
        in_specs=placed,
        out_specs=(
            P(("row", "col"), None),
            P(("row", "col"), None),
            P(("col", "row"), None),
            P(("col", "row"), None),
        ),
        check_vma=False,
    )
```

profile of v0, /device:TPU:0, one launch (start us, length us, event | category | flops | bytes accessed | tf_op | source)
XLA Modules:
  0.0 125.1 jit_solution(8723393421460927545)
XLA Ops:
  1.3 0.8 copy.11.pair_ref
  2.0 0.0 copy-start
  2.0 1.6 %copy-done = s32[1,32,128,128]{3,2,1,0:T(8,128)S(1)} copy-done((s32[1,32,128,128]{3,2,1,0:T(8,128)S(1)}, s32[1,32,128,128]{3,2,1,0:T(8,128)}, u32[]{:S(2)}) %copy-start) | copy-done | bytes 2097176
  3.6 0.0 copy-start.4
  3.6 0.9 copy-done.4
  4.6 0.0 copy-start.5
  4.6 0.9 copy-done.5
  5.5 0.0 copy-start.6
  5.5 0.9 copy-done.6
  6.4 0.0 copy-start.7
  6.4 0.9 copy-done.7
  7.3 3.7 %shard_map.102 = (bf16[16,96,128]{2,1,0:T(8,128)(2,1)S(1)}, bf16[16,96,128]{2,1,0:T(8,128)(2,1)S(1)}, f32[8,4,128,128]{3,2,1,0:T(8,128)S(1)}) custom-call(s32[32,2]{1,0:T(8,128)S(1)} %copy.11.pair_ref, s32[1]{0:T(128)S(6)} %copy.16.count_ref, bf16[128,768]{1,0:T(8,128)(2,1)S(1)} %copy-done.4, bf16[128,768]{1,0:T(8,128)(2,1)S(1)} %copy-done.5, ...), custom_call_target="tpu_custom_call" | custom-call | tf_op jit(solution)/shard_map/pallas_call | solution.py:499
  11.1 0.0 copy-start.1
  11.1 1.3 %copy-done.1 = f32[8,4,128,128]{3,2,1,0:T(8,128)} copy-done((f32[8,4,128,128]{3,2,1,0:T(8,128)}, f32[8,4,128,128]{3,2,1,0:T(8,128)S(1)}, u32[]{:S(2)}) %copy-start.1) | copy-done | bytes 2097176
  12.4 0.0 copy-start.2
  12.4 0.7 copy-done.2
  13.2 0.0 copy-start.3
  13.2 0.7 copy-done.3
  13.9 104.7 %shard_map.103 = (bf16[8,96,128]{2,1,0:T(8,128)(2,1)}, f32[8,96,128]{2,1,0:T(8,128)}, f32[8,96,128]{2,1,0:T(8,128)}, f32[8,96,128]{2,1,0:T(8,128)}) custom-call(bf16[16,96,128]{2,1,0:T(8,128)(2,1)} %copy-done.2, bf16[16,96,128]{2,1,0:T(8,128)(2,1)} %copy-done.3, f32[8,4,128,128]{3,2,1,0:T(8,128)} %copy-done.1), custom_call_target="tpu_custom_call" | custom-call | tf_op jit(solution)/shard_map/pallas_call | solution.py:512
  118.6 0.0 copy-start.8
  118.6 1.8 %copy.12 = bf16[768,128]{0,1:T(8,128)(2,1)} copy(bf16[768,128]{1,0:T(8,128)(2,1)} %bitcast.18) | data formatting | bytes 393216 | tf_op jit(solution)/shard_map/reshape | solution.py:557
  120.4 1.9 %copy.13 = f32[768,128]{0,1:T(8,128)} copy(f32[768,128]{1,0:T(8,128)} %bitcast.16) | data formatting | bytes 786432 | tf_op jit(solution)/shard_map/reshape | solution.py:557
  122.3 1.9 %copy.14 = f32[768,128]{0,1:T(8,128)} copy(f32[768,128]{1,0:T(8,128)} %bitcast.15) | data formatting | bytes 786432 | tf_op jit(solution)/shard_map/reshape | solution.py:557
  124.2 0.0 copy-done.8
  124.2 0.9 copy.15
Async XLA Ops:
  2.0 1.6 %copy-start = (s32[1,32,128,128]{3,2,1,0:T(8,128)S(1)}, s32[1,32,128,128]{3,2,1,0:T(8,128)}, u32[]{:S(2)}) copy-start(s32[1,32,128,128]{3,2,1,0:T(8,128)} %param.13) | copy-start | bytes 6291460
  3.6 0.9 copy-start.4
  4.6 0.9 copy-start.5
  5.5 0.9 copy-start.6
  6.4 0.9 copy-start.7
  11.1 1.3 %copy-start.1 = (f32[8,4,128,128]{3,2,1,0:T(8,128)}, f32[8,4,128,128]{3,2,1,0:T(8,128)S(1)}, u32[]{:S(2)}) copy-start(f32[8,4,128,128]{3,2,1,0:T(8,128)S(1)} %get-tuple-element.13.bias_ref) | copy-start | bytes 6291460
  12.4 0.7 copy-start.2
  13.2 0.7 copy-start.3
  118.6 5.6 %copy-start.8 = (f32[8,96,128]{2,1,0:T(8,128)S(1)}, f32[8,96,128]{2,1,0:T(8,128)}, u32[]{:S(2)}) copy-start(f32[8,96,128]{2,1,0:T(8,128)} %get-tuple-element.17) | copy-start | bytes 1179652
where the time goes:
time: 125 us
  Pallas kernels  108 us (86%)
  local copies, waits for them, and re-layouts  15.4 us (12%)
  between operations  1.32 us (1%)
    pallas_call x1, Pallas kernels, fused(): pl.pallas_call(functools.partial(layer_kernel, n_ring), out_shape=(jax.Sh...  105 us
    unnamed x18, local copies, waits for them, and re-layouts  8.12 us
    reshape x4, local copies, waits for them, and re-layouts, fused(): out.reshape(HEADS * HEAD_DIM, BLOCK)  6.52 us
    pallas_call x1, Pallas kernels, fused(): pl.pallas_call(prepare_kernel, out_shape=(jax.ShapeDtypeStruct(block, jnp...  3.75 us

commit v1 on v0

--- a/solution.py
+++ b/solution.py
@@ -170,29 +170,40 @@
     )
 
 
-def prepare_kernel(pair_ref, count_ref, q_ref, k_ref, v_ref, g_ref, mask_ref, qg_ref, kv_ref, bias_ref):
-    for src, dst, first in ((q_ref, qg_ref, 0), (g_ref, qg_ref, HEADS), (k_ref, kv_ref, 0), (v_ref, kv_ref, HEADS)):
-        turned = jnp.transpose(src[...].astype(jnp.float32)).astype(jnp.bfloat16)
-        dst[first : first + HEADS] = turned.reshape(HEADS, HEAD_DIM, BLOCK)
-    bias_ref[...] = jnp.full(bias_ref.shape, MASKED, jnp.float32)
-
-    @pl.loop(0, count_ref[0])
-    def _(slot):
-        target = pair_ref[slot, 0]
-        source = pair_ref[slot, 1]
-        kept = jnp.transpose(mask_ref[slot].astype(jnp.float32))
-        bias_ref[source, target] = jnp.where(kept > 0.5, 0.0, MASKED)
+def write_kernel(*refs):
+    count = (len(refs) - 2) // 3
+    ins, outs, held = refs[:count], refs[count : 2 * count], refs[2 * count : 3 * count]
+    read_sem, write_sem = refs[3 * count :]
+    reads = [pltpu.make_async_copy(ins[k], held[k], read_sem.at[k]) for k in range(count)]
+    writes = [pltpu.make_async_copy(held[k], outs[k], write_sem.at[k]) for k in range(count)]
+    for copy in reads:
+        copy.start()
+    for k in range(count):
+        reads[k].wait()
+        writes[k].start()
+    for copy in writes:
+        copy.wait()
 
 
 def layer_kernel(
     n_ring,
-    qg_own,
-    kv_own,
-    bias_ref,
+    pair_ref,
+    count_ref,
+    q_ref,
+    k_ref,
+    v_ref,
+    g_ref,
+    mask_ref,
     att_ref,
     qgrad_ref,
     kgrad_ref,
     vgrad_ref,
+    raw_buf,
+    mask_buf,
+    bias_ref,
+    qg_own,
+    att_buf,
+    grad_bufs,
     kv_buf,
     qg_buf,
     weight_buf,
@@ -222,6 +233,8 @@
     col_send,
     col_recv,
     own_sem,
+    load_sem,
+    save_sem,
 ):
     scale = HEAD_DIM ** (-0.5)
     row = lax.axis_index("row")
@@ -256,39 +269,63 @@
         pending.append(copy)
         return copy
 
+    loads = [
+        pltpu.make_async_copy(ref, raw_buf.at[k], load_sem.at[k])
+        for k, ref in enumerate((k_ref, v_ref, q_ref, g_ref))
+    ]
+    loads.append(pltpu.make_async_copy(mask_ref, mask_buf, load_sem.at[4]))
+    for load in loads:
+        load.start()
     barrier = pltpu.get_barrier_semaphore()
     for device in [right, left] + others:
         pl.semaphore_signal(barrier, inc=1, device_id=device, device_id_type=MESH)
+
+    def turn(index):
+        loads[index].wait()
+        turned = jnp.transpose(raw_buf[index].astype(jnp.float32)).astype(jnp.bfloat16)
+        return turned.reshape(HEADS, HEAD_DIM, BLOCK)
+
+    kv_buf[0, 0:HEADS] = turn(0)
+    kv_buf[0, HEADS:] = turn(1)
     pl.semaphore_wait(barrier, 5)
 
     def lanes(index):
         return pl.ds(pl.multiple_of(index * BLOCK, BLOCK), BLOCK)
 
-    def ring_right(step):
-        part = pl.ds(0, 2 * HEADS if step < half_ring else HEADS)
-        src = kv_own if step == 1 else kv_buf.at[step - 1]
+    def ring_part(step, way, part):
+        first = HEADS * (part ^ way)
+        at = pl.ds(first, HEADS)
+        at_sem = (2 * (step - 1) + part) * 2 + way
+        src = (step - 1, (n_ring - step + 1) % n_ring)[way]
+        dst = (step, n_ring - step)[way]
         return send(
-            src.at[part], kv_buf.at[step, part], ring_send.at[step], ring_recv.at[step], right
-        )
-
-    def ring_left(step):
-        part = pl.ds(0, 2 * HEADS) if step < half_ring else pl.ds(HEADS, HEADS)
-        src = kv_own if step == 1 else kv_buf.at[n_ring - step + 1]
-        return send(
-            src.at[part],
-            kv_buf.at[n_ring - step, part],
-            ring_send.at[half_ring + step],
-            ring_recv.at[half_ring + step],
-            left,
-        )
-
+            kv_buf.at[src, at],
+            kv_buf.at[dst, at],
+            ring_send.at[at_sem],
+            ring_recv.at[at_sem],
+            (right, left)[way],
+        )
+
+    coming = [[ring_part(1, way, part) for way in range(2)] for part in range(2)]
+    qg_own[0:HEADS] = turn(2)
+    qg_own[HEADS:] = turn(3)
     from_chip = send(qg_own, qg_buf.at[:, :, lanes(col)], qg_send.at[0], qg_recv.at[0], chip_peer)
     from_core = send(qg_own, qg_buf.at[:, :, lanes(col)], qg_send.at[1], qg_recv.at[1], core_peer)
-    on_right = ring_right(1)
-    on_left = ring_left(1)
     own_copy = pltpu.make_async_copy(qg_own, qg_buf.at[:, :, lanes(col)], own_sem.at[0])
     own_copy.start()
-    kv_buf[0] = kv_own[...]
+    loads[4].wait()
+
+    @pl.loop(0, bias_ref.shape[0] * bias_ref.shape[1])
+    def _(cell):
+        source, target = cell // bias_ref.shape[1], cell % bias_ref.shape[1]
+        slot, live = jnp.int32(0), jnp.int32(0)
+        for t in range(mask_buf.shape[0]):
+            hit = (pair_ref[0, t] == target) & (pair_ref[1, t] == source) & (t < count_ref[0])
+            slot = jnp.where(hit, t, slot)
+            live = jnp.where(hit, 1, live)
+        kept = jnp.transpose((mask_buf[slot] * live).astype(jnp.float32))
+        bias_ref[source, target] = jnp.where(kept > 0.5, 0.0, MASKED)
+
     own_copy.wait()
     from_chip.wait_recv()
     passed = send(
@@ -326,19 +363,20 @@
                 chunk_stats[slot, head, 1:2, cut] = jnp.sum(weights, axis=0, keepdims=True)
                 chunk_stats[slot, head, 2:3, cut] = jnp.sum(weights * dots, axis=0, keepdims=True)
 
-    stats_of(0)
+    ready = [0]
     for step in range(1, half_ring + 1):
-        on_right.wait_recv()
-        last_right = on_right
-        if step < half_ring:
-            on_right = ring_right(step + 1)
-        on_left.wait_recv()
-        if step < half_ring:
-            on_left = ring_left(step + 1)
-            stats_of(step)
-            stats_of(n_ring - step)
-        else:
-            stats_of(step)
+        for part in range(2 if step < half_ring else 1):
+            for way in range(2):
+                coming[part][way].wait_recv()
+                if step + 1 < half_ring or (step + 1 == half_ring and part == 0):
+                    coming[part][way] = ring_part(step + 1, way, part)
+            if ready:
+                stats_of(ready.pop(0))
+        while ready:
+            stats_of(ready.pop(0))
+        ready = [step, n_ring - step] if step < half_ring else [step]
+    for slot in ready:
+        stats_of(slot)
 
     @pl.loop(0, HEADS)
     def _(head):
@@ -381,7 +419,7 @@
                 jnp.exp(chunk_stats[slot, head, 0:1] - top) * inverse
             )
 
-    def grads_of(slot):
+    def grads_of(slot, held):
         @pl.loop(0, HEADS)
         def _(head):
             key_t = kv_buf[slot, head]
@@ -399,48 +437,54 @@
                 value_part += contract(qg_buf[HEADS + head, :, cut], probs, 1, 1)
                 acc_buf[head, :, cut] += contract(key_t, score_grads, 1, 0)
                 acc_buf[HEADS + head, :, cut] += contract(value_t, probs, 1, 0)
-            part_buf[head] = key_part
-            part_buf[HEADS + head] = value_part
-
-    def pass_on(outgoing, incoming, hop, sems, device, arrived, first, count):
+            part_buf[held, head] = key_part
+            part_buf[held, HEADS + head] = value_part
+
+    sums = {}
+
+    def pass_on(hop, way, part, held):
+        outgoing = (right_out, left_out)[way]
+        incoming = (right_in, left_in)[way]
+        first = HEADS * (part ^ way)
+        arrived = sums.get((hop - 1, way, part))
         if arrived is not None:
             arrived.wait_recv()
 
-        @pl.loop(first, first + count)
+        @pl.loop(first, first + HEADS)
         def _(index):
-            term = part_buf[index]
+            term = part_buf[held, index]
             if arrived is not None:
-                if hop == 1:
-                    known = index < HEADS if sems == 0 else index >= HEADS
-                    before = incoming[0, index].astype(jnp.float32)
-                    term = term + jnp.where(known, before, 0.0)
-                else:
-                    term = term + incoming[hop - 1, index].astype(jnp.float32)
+                term = term + incoming[hop - 1, index].astype(jnp.float32)
             outgoing[hop, index] = term.astype(jnp.bfloat16)
 
-        at = pl.ds(first, count)
-        return send(
+        at = pl.ds(first, HEADS)
+        at_sem = (2 * hop + part) * 2 + way
+        sums[hop, way, part] = send(
             outgoing.at[hop, at],
             incoming.at[hop, at],
-            sum_send.at[sems * half_ring + hop],
-            sum_recv.at[sems * half_ring + hop],
-            device,
-        )
-
-    def clear(ref, first):
-        ref[0, pl.ds(first, HEADS)] = jnp.zeros((HEADS, HEAD_DIM, BLOCK), jnp.bfloat16)
-
-    clear(right_in, HEADS)
-    clear(left_in, 0)
-    grads_of(half_ring)
-    to_right = pass_on(right_out, right_in, 0, 0, right, None, 0, HEADS)
-    to_left = pass_on(left_out, left_in, 0, 1, left, None, HEADS, HEADS)
-    for hop in range(1, half_ring):
-        grads_of(half_ring + hop)
-        to_right = pass_on(right_out, right_in, hop, 0, right, to_right, 0, 2 * HEADS)
-        grads_of(half_ring - hop)
-        to_left = pass_on(left_out, left_in, hop, 1, left, to_left, 0, 2 * HEADS)
-    grads_of(0)
+            sum_send.at[at_sem],
+            sum_recv.at[at_sem],
+            (right, left)[way],
+        )
+
+    last = half_ring - 1
+    grads_of(half_ring, 0)
+    pass_on(0, 0, 0, 0)
+    pass_on(0, 1, 0, 0)
+    grads_of(half_ring + 1, 2)
+    grads_of(half_ring - 1, 3)
+    for hop in range(1, last):
+        now, later = 2 * (hop % 2), 2 * ((hop + 1) % 2)
+        pass_on(hop, 0, 0, now)
+        pass_on(hop, 1, 0, now + 1)
+        grads_of(half_ring + hop + 1, later)
+        pass_on(hop, 0, 1, now)
+        pass_on(hop, 1, 1, now + 1)
+        grads_of(half_ring - hop - 1, later + 1)
+    now, own = 2 * (last % 2), 2 * ((last + 1) % 2)
+    pass_on(last, 0, 0, now)
+    pass_on(last, 1, 0, now + 1)
+    grads_of(0, own)
 
     @pl.loop(0, 2 * HEADS)
     def _(index):
@@ -449,6 +493,8 @@
 
     far = send(core_out.at[1], core_in.at[1], col_send.at[1], col_recv.at[1], core_peer)
     near = send(core_out.at[0], core_in.at[0], col_send.at[0], col_recv.at[0], core_peer)
+    pass_on(last, 0, 1, now)
+    pass_on(last, 1, 1, now + 1)
     far.wait_recv()
 
     @pl.loop(0, 2 * HEADS)
@@ -459,67 +505,73 @@
 
     across = send(chip_out, chip_in, col_send.at[2], col_recv.at[2], chip_peer)
     near.wait_recv()
-    to_right.wait_recv()
-    to_left.wait_recv()
-
-    @pl.loop(0, HEADS)
-    def _(head):
-        for first, ref in ((0, kgrad_ref), (HEADS, vgrad_ref)):
-            index = head + first
-            ref[head] = (
-                part_buf[index]
-                + right_in[half_ring - 1, index].astype(jnp.float32)
-                + left_in[half_ring - 1, index].astype(jnp.float32)
-            )
+
+    def summed(first):
+        at = pl.ds(first, HEADS)
+        return (
+            acc_buf[at, :, lanes(col)]
+            + core_in[0, at].astype(jnp.float32)
+            + chip_in[at].astype(jnp.float32)
+        )
+
+    def natural(value):
+        return jnp.transpose(value.reshape(HEADS * HEAD_DIM, BLOCK))
+
+    saves = []
+
+    def save(src, dst):
+        copy = pltpu.make_async_copy(src, dst, save_sem.at[len(saves)])
+        copy.start()
+        saves.append(copy)
+
+    for way in range(2):
+        for part in range(2):
+            sums[last, way, part].wait_recv()
+    for k, ref in ((0, kgrad_ref), (1, vgrad_ref)):
+        at = pl.ds(k * HEADS, HEADS)
+        grad_bufs[k] = natural(
+            part_buf[own, at]
+            + right_in[half_ring - 1, at].astype(jnp.float32)
+            + left_in[half_ring - 1, at].astype(jnp.float32)
+        )
+        save(grad_bufs.at[k], ref)
 
     across.wait_recv()
-
-    @pl.loop(0, HEADS)
-    def _(head):
-        def summed(index):
-            return (
-                acc_buf[index, :, lanes(col)]
-                + core_in[0, index].astype(jnp.float32)
-                + chip_in[index].astype(jnp.float32)
-            )
-
-        qgrad_ref[head] = summed(head)
-        att_ref[head] = summed(HEADS + head).astype(jnp.bfloat16)
-
+    grad_bufs[2] = natural(summed(0))
+    save(grad_bufs.at[2], qgrad_ref)
+    att_buf[...] = natural(summed(HEADS)).astype(jnp.bfloat16)
+    save(att_buf, att_ref)
+    for copy in saves:
+        copy.wait()
     for copy in pending:
         copy.wait_send()
 
 
 def fused(n_ring, n_col, queries, key_rows, values, out_grad, block_pairs, pair_count, edge_mask):
-    vmem = pl.BlockSpec(memory_space=pltpu.VMEM)
     smem = pl.BlockSpec(memory_space=pltpu.SMEM)
+    placed = pl.BlockSpec(memory_space=pl.ANY)
     block = (2 * HEADS, HEAD_DIM, BLOCK)
     wide = n_col * BLOCK
-    flat = (HEADS, HEAD_DIM, BLOCK)
-    qg_own, kv_own, bias = pl.pallas_call(
-        prepare_kernel,
-        out_shape=(
-            jax.ShapeDtypeStruct(block, jnp.bfloat16),
-            jax.ShapeDtypeStruct(block, jnp.bfloat16),
-            jax.ShapeDtypeStruct((n_ring, n_col, BLOCK, BLOCK), jnp.float32),
-        ),
-        in_specs=[smem] * 2 + [vmem] * 5,
-        out_specs=(vmem, vmem, vmem),
-        compiler_params=pltpu.CompilerParams(vmem_limit_bytes=24 * 2**20),
-    )(block_pairs[0], pair_count, queries, key_rows, values, out_grad, edge_mask[0])
+    rows, features = queries.shape
+    slots = edge_mask.shape[1]
     half = n_ring // 2
     dma = pltpu.SemaphoreType.DMA
+    shapes = tuple(
+        jax.ShapeDtypeStruct((rows, features), kind)
+        for kind in (jnp.bfloat16, jnp.float32, jnp.float32, jnp.float32)
+    )
     outs = pl.pallas_call(
         functools.partial(layer_kernel, n_ring),
-        out_shape=(
-            jax.ShapeDtypeStruct(flat, jnp.bfloat16),
-            jax.ShapeDtypeStruct(flat, jnp.float32),
-            jax.ShapeDtypeStruct(flat, jnp.float32),
-            jax.ShapeDtypeStruct(flat, jnp.float32),
-        ),
-        in_specs=[vmem] * 3,
-        out_specs=(vmem,) * 4,
+        out_shape=shapes,
+        in_specs=[smem] * 2 + [placed] * 5,
+        out_specs=(placed,) * 4,
         scratch_shapes=[
+            pltpu.VMEM((4, rows, features), jnp.bfloat16),
+            pltpu.VMEM((slots, BLOCK, BLOCK), jnp.int32),
+            pltpu.VMEM((n_ring, n_col, BLOCK, BLOCK), jnp.float32),
+            pltpu.VMEM(block, jnp.bfloat16),
+            pltpu.VMEM((rows, features), jnp.bfloat16),
+            pltpu.VMEM((3, rows, features), jnp.float32),
             pltpu.VMEM((n_ring,) + block, jnp.bfloat16),
             pltpu.VMEM((2 * HEADS, HEAD_DIM, wide), jnp.bfloat16),
             pltpu.VMEM((n_ring, HEADS, BLOCK, wide), jnp.float32),
@@ -529,7 +581,7 @@
             pltpu.VMEM((HEADS, n_ring, wide), jnp.float32),
             pltpu.VMEM((HEADS, 8, wide), jnp.float32),
             pltpu.VMEM((2 * HEADS, HEAD_DIM, wide), jnp.float32),
-            pltpu.VMEM(block, jnp.float32),
+            pltpu.VMEM((4,) + block, jnp.float32),
             pltpu.VMEM((half,) + block, jnp.bfloat16),
             pltpu.VMEM((half,) + block, jnp.bfloat16),
             pltpu.VMEM((half,) + block, jnp.bfloat16),
@@ -538,23 +590,33 @@
             pltpu.VMEM((2,) + block, jnp.bfloat16),
             pltpu.VMEM(block, jnp.bfloat16),
             pltpu.VMEM(block, jnp.bfloat16),
-            dma((2 * half + 1,)),
-            dma((2 * half + 1,)),
+            dma((4 * half,)),
+            dma((4 * half,)),
             dma((3,)),
             dma((3,)),
             dma((4,)),
             dma((4,)),
-            dma((2 * half,)),
-            dma((2 * half,)),
+            dma((4 * half,)),
+            dma((4 * half,)),
             dma((3,)),
             dma((3,)),
             dma((1,)),
+            dma((5,)),
+            dma((4,)),
         ],
         compiler_params=pltpu.CompilerParams(
-            collective_id=0, has_side_effects=True, vmem_limit_bytes=60 * 2**20
+            collective_id=0, has_side_effects=True, vmem_limit_bytes=61 * 2**20
         ),
-    )(qg_own, kv_own, bias)
-    return tuple(jnp.transpose(out.reshape(HEADS * HEAD_DIM, BLOCK)) for out in outs)
+    )(jnp.transpose(block_pairs[0]), pair_count, queries, key_rows, values, out_grad, edge_mask[0])
+    return pl.pallas_call(
+        write_kernel,
+        out_shape=shapes,
+        in_specs=[placed] * 4,
+        out_specs=(placed,) * 4,
+        scratch_shapes=[pltpu.VMEM(shape.shape, shape.dtype) for shape in shapes]
+        + [dma((4,)), dma((4,))],
+        compiler_params=pltpu.CompilerParams(vmem_limit_bytes=61 * 2**20),
+    )(*outs)
 
 
 def solution(mesh):

time: 125 us -> 97 us (0.78)
  local copies, waits for them, and re-layouts: 15.4 us -> 0 us
  Pallas kernels: 108 us -> 95.5 us
    pallas_call x2, Pallas kernels: 108 us -> 95.5 us  [the longest x1 93.4 us: fused(): pl.pallas_call(functools.partial(layer_kernel, n_ring), out_shape=shapes,...]
    unnamed x18 -> x0, local copies, waits for them, and re-layouts: 8.12 us -> none
    reshape x4 -> x0, local copies, waits for them, and re-layouts: 6.52 us -> none  [fused(): out.reshape(HEADS * HEAD_DIM, BLOCK)]
where the time goes in v1:
time: 97 us; the launch traced here: 96.8 us
  Pallas kernels  95.5 us (98%)
  between operations  1.29 us (1%)
    pallas_call x1, Pallas kernels, fused(): pl.pallas_call(functools.partial(layer_kernel, n_ring), out_shape=shapes,...  93.4 us
    pallas_call x1, Pallas kernels, fused(): pl.pallas_call(write_kernel, out_shape=shapes, in_specs=[placed] * 4, out...  2.18 us

profile of v1, /device:TPU:0, one launch (start us, length us, event | category | flops | bytes accessed | tf_op | source)
XLA Modules:
  0.0 96.8 jit_solution(13291632571948514049)
XLA Ops:
  1.3 93.4 %shard_map.102 = (bf16[128,768]{1,0:T(8,128)(2,1)}, f32[128,768]{1,0:T(8,128)}, f32[128,768]{1,0:T(8,128)}, f32[128,768]{1,0:T(8,128)}) custom-call(s32[2,32]{1,0:T(2,128)} %bitcast.5, s32[1]{0:T(128)S(6)} %copy.11.count_ref, bf16[128,768]{1,0:T(8,128)(2,1)} %q_ref.1, bf16[128,768]{1,0:T(8,128)(2,1)} %k_ref.1, bf16[128,768]{1,0:T(8,128)(2,1)} %v_ref.1, ...), custom_call_target="tpu_custom_call" | custom-call | tf_op jit(solution)/shard_map/pallas_call | solution.py:563
  94.6 2.2 %shard_map.103 = (bf16[128,768]{1,0:T(8,128)(2,1)}, f32[128,768]{1,0:T(8,128)}, f32[128,768]{1,0:T(8,128)}, f32[128,768]{1,0:T(8,128)}) custom-call(bf16[128,768]{1,0:T(8,128)(2,1)} %get-tuple-element.8.refs_0_, f32[128,768]{1,0:T(8,128)} %get-tuple-element.9.refs_1_, f32[128,768]{1,0:T(8,128)} %get-tuple-element.10.refs_2_, ...), custom_call_target="tpu_custom_call" | custom-call | tf_op jit(solution)/shard_map/pallas_call | solution.py:611

commit v2 on v1

--- a/solution.py
+++ b/solution.py
@@ -159,6 +159,8 @@
 MASKED = -1e30
 FLOOR = -1e28
 MESH = pl.DeviceIdType.MESH
+PIECES = 4
+LOG2_E = 1.4426950408889634
 
 
 def contract(left, right, left_dim, right_dim):
@@ -237,6 +239,7 @@
     save_sem,
 ):
     scale = HEAD_DIM ** (-0.5)
+    group = 2 * HEADS // PIECES
     row = lax.axis_index("row")
     col = lax.axis_index("col")
     half_ring = n_ring // 2
@@ -293,9 +296,8 @@
         return pl.ds(pl.multiple_of(index * BLOCK, BLOCK), BLOCK)
 
     def ring_part(step, way, part):
-        first = HEADS * (part ^ way)
-        at = pl.ds(first, HEADS)
-        at_sem = (2 * (step - 1) + part) * 2 + way
+        at = pl.ds((group * part + HEADS * way) % (2 * HEADS), group)
+        at_sem = (PIECES * (step - 1) + part) * 2 + way
         src = (step - 1, (n_ring - step + 1) % n_ring)[way]
         dst = (step, n_ring - step)[way]
         return send(
@@ -306,7 +308,7 @@
             (right, left)[way],
         )
 
-    coming = [[ring_part(1, way, part) for way in range(2)] for part in range(2)]
+    coming = [[ring_part(1, way, part) for way in range(2)] for part in range(PIECES)]
     qg_own[0:HEADS] = turn(2)
     qg_own[HEADS:] = turn(3)
     from_chip = send(qg_own, qg_buf.at[:, :, lanes(col)], qg_send.at[0], qg_recv.at[0], chip_peer)
@@ -341,10 +343,11 @@
     width = 2 * BLOCK
     parts = qg_buf.shape[2] // width
 
-    def stats_of(slot):
+    def stats_of(slot, piece):
         source = row_at(place - slot)
-
-        @pl.loop(0, HEADS)
+        few = HEADS // PIECES * 2
+
+        @pl.loop(piece * few, piece * few + few, unroll=2)
         def _(head):
             key_t = kv_buf[slot, head]
             value_t = kv_buf[slot, HEADS + head]
@@ -353,45 +356,47 @@
                 bias = jnp.concatenate(
                     [bias_ref[source, 2 * part], bias_ref[source, 2 * part + 1]], axis=1
                 )
-                scores = contract(key_t, qg_buf[head, :, cut], 0, 0) * scale + bias
+                scores = contract(key_t, qg_buf[head, :, cut], 0, 0) * (scale * LOG2_E) + bias
                 dots = contract(value_t, qg_buf[HEADS + head, :, cut], 0, 0)
                 top = jnp.maximum(jnp.max(scores, axis=0, keepdims=True), FLOOR)
-                weights = jnp.exp(scores - top)
+                weights = jnp.exp2(scores - top)
                 weight_buf[slot, head, :, cut] = weights
                 dots_buf[slot, head, :, cut] = dots
-                chunk_stats[slot, head, 0:1, cut] = top
-                chunk_stats[slot, head, 1:2, cut] = jnp.sum(weights, axis=0, keepdims=True)
-                chunk_stats[slot, head, 2:3, cut] = jnp.sum(weights * dots, axis=0, keepdims=True)
-
-    ready = [0]
+                at = pl.ds(head, 1)
+                chunk_stats[slot, 0, at, cut] = top
+                chunk_stats[slot, 1, at, cut] = jnp.sum(weights, axis=0, keepdims=True)
+                chunk_stats[slot, 2, at, cut] = jnp.sum(weights * dots, axis=0, keepdims=True)
+
+    work = PIECES // 2
+    ready = [(0, piece) for piece in range(work)]
     for step in range(1, half_ring + 1):
-        for part in range(2 if step < half_ring else 1):
+        pieces = PIECES if step < half_ring else PIECES // 2
+        for part in range(pieces):
             for way in range(2):
                 coming[part][way].wait_recv()
-                if step + 1 < half_ring or (step + 1 == half_ring and part == 0):
+                if step + 1 < half_ring or (step + 1 == half_ring and part < PIECES // 2):
                     coming[part][way] = ring_part(step + 1, way, part)
             if ready:
-                stats_of(ready.pop(0))
+                stats_of(*ready.pop(0))
         while ready:
-            stats_of(ready.pop(0))
-        ready = [step, n_ring - step] if step < half_ring else [step]
-    for slot in ready:
-        stats_of(slot)
-
-    @pl.loop(0, HEADS)
-    def _(head):
-        top = chunk_stats[0, head, 0:1]
-        for slot in range(1, n_ring):
-            top = jnp.maximum(top, chunk_stats[slot, head, 0:1])
-        total = jnp.zeros_like(top)
-        mixed = jnp.zeros_like(top)
-        for slot in range(n_ring):
-            factor = jnp.exp(chunk_stats[slot, head, 0:1] - top)
-            total = total + factor * chunk_stats[slot, head, 1:2]
-            mixed = mixed + factor * chunk_stats[slot, head, 2:3]
-        stat_buf[0, head, 0:1] = top
-        stat_buf[0, head, 1:2] = total
-        stat_buf[0, head, 2:3] = mixed
+            stats_of(*ready.pop(0))
+        slots = [step, n_ring - step] if step < half_ring else [step]
+        ready = [(slot, piece) for slot in slots for piece in range(work)]
+    for item in ready:
+        stats_of(*item)
+
+    top = chunk_stats[0, 0]
+    for slot in range(1, n_ring):
+        top = jnp.maximum(top, chunk_stats[slot, 0])
+    total = jnp.zeros_like(top)
+    mixed = jnp.zeros_like(top)
+    for slot in range(n_ring):
+        factor = jnp.exp2(chunk_stats[slot, 0] - top)
+        total = total + factor * chunk_stats[slot, 1]
+        mixed = mixed + factor * chunk_stats[slot, 2]
+    stat_buf[0, 0] = top
+    stat_buf[0, 1] = total
+    stat_buf[0, 2] = mixed
 
     shared = [
         send(stat_buf.at[0], stat_buf.at[k], stat_send.at[k], stat_recv.at[k], others[k - 1])
@@ -401,26 +406,24 @@
     for copy in shared:
         copy.wait_recv()
 
-    @pl.loop(0, HEADS)
-    def _(head):
-        top = stat_buf[0, head, 0:1]
-        for k in range(1, 4):
-            top = jnp.maximum(top, stat_buf[k, head, 0:1])
-        total = jnp.zeros_like(top)
-        mixed = jnp.zeros_like(top)
-        for k in range(4):
-            factor = jnp.exp(stat_buf[k, head, 0:1] - top)
-            total = total + factor * stat_buf[k, head, 1:2]
-            mixed = mixed + factor * stat_buf[k, head, 2:3]
-        inverse = 1.0 / total
-        delta_buf[head, 0:1] = mixed * inverse
-        for slot in range(n_ring):
-            factor_buf[head, slot : slot + 1] = (
-                jnp.exp(chunk_stats[slot, head, 0:1] - top) * inverse
-            )
-
-    def grads_of(slot, held):
-        @pl.loop(0, HEADS)
+    top = stat_buf[0, 0]
+    for k in range(1, 4):
+        top = jnp.maximum(top, stat_buf[k, 0])
+    total = jnp.zeros_like(top)
+    mixed = jnp.zeros_like(top)
+    for k in range(4):
+        factor = jnp.exp2(stat_buf[k, 0] - top)
+        total = total + factor * stat_buf[k, 1]
+        mixed = mixed + factor * stat_buf[k, 2]
+    inverse = 1.0 / total
+    delta_buf[...] = mixed * inverse
+    for slot in range(n_ring):
+        factor_buf[slot] = jnp.exp2(chunk_stats[slot, 0] - top) * inverse
+
+    def grads_of(slot, held, piece):
+        few = HEADS // PIECES * 2
+
+        @pl.loop(piece * few, piece * few + few, unroll=2)
         def _(head):
             key_t = kv_buf[slot, head]
             value_t = kv_buf[slot, HEADS + head]
@@ -428,9 +431,9 @@
             value_part = jnp.zeros((HEAD_DIM, BLOCK), jnp.float32)
             for part in range(parts):
                 cut = pl.ds(part * width, width)
-                probs = weight_buf[slot, head, :, cut] * factor_buf[head, slot : slot + 1, cut]
+                probs = weight_buf[slot, head, :, cut] * factor_buf[slot, pl.ds(head, 1), cut]
                 score_grads = (
-                    probs * (dots_buf[slot, head, :, cut] - delta_buf[head, 0:1, cut]) * scale
+                    probs * (dots_buf[slot, head, :, cut] - delta_buf[pl.ds(head, 1), cut]) * scale
                 ).astype(jnp.bfloat16)
                 probs = probs.astype(jnp.bfloat16)
                 key_part += contract(qg_buf[head, :, cut], score_grads, 1, 1)
@@ -445,20 +448,20 @@
     def pass_on(hop, way, part, held):
         outgoing = (right_out, left_out)[way]
         incoming = (right_in, left_in)[way]
-        first = HEADS * (part ^ way)
+        first = (group * part + HEADS * way) % (2 * HEADS)
         arrived = sums.get((hop - 1, way, part))
         if arrived is not None:
             arrived.wait_recv()
 
-        @pl.loop(first, first + HEADS)
+        @pl.loop(first, first + group)
         def _(index):
             term = part_buf[held, index]
             if arrived is not None:
                 term = term + incoming[hop - 1, index].astype(jnp.float32)
             outgoing[hop, index] = term.astype(jnp.bfloat16)
 
-        at = pl.ds(first, HEADS)
-        at_sem = (2 * hop + part) * 2 + way
+        at = pl.ds(first, group)
+        at_sem = (PIECES * hop + part) * 2 + way
         sums[hop, way, part] = send(
             outgoing.at[hop, at],
             incoming.at[hop, at],
@@ -468,23 +471,37 @@
         )
 
     last = half_ring - 1
-    grads_of(half_ring, 0)
-    pass_on(0, 0, 0, 0)
-    pass_on(0, 1, 0, 0)
-    grads_of(half_ring + 1, 2)
-    grads_of(half_ring - 1, 3)
+    for piece in range(work):
+        grads_of(half_ring, 0, piece)
+        pass_on(0, 0, piece, 0)
+        pass_on(0, 1, piece, 0)
+    for piece in range(work):
+        grads_of(half_ring + 1, 2, piece)
+        grads_of(half_ring - 1, 3, piece)
     for hop in range(1, last):
         now, later = 2 * (hop % 2), 2 * ((hop + 1) % 2)
-        pass_on(hop, 0, 0, now)
-        pass_on(hop, 1, 0, now + 1)
-        grads_of(half_ring + hop + 1, later)
-        pass_on(hop, 0, 1, now)
-        pass_on(hop, 1, 1, now + 1)
-        grads_of(half_ring - hop - 1, later + 1)
+        todo = [
+            (slot, held, piece)
+            for piece in range(work)
+            for slot, held in (
+                (half_ring + hop + 1, later),
+                (half_ring - hop - 1, later + 1),
+            )
+        ]
+        for part in range(PIECES):
+            pass_on(hop, 0, part, now)
+            pass_on(hop, 1, part, now + 1)
+            if todo:
+                grads_of(*todo.pop(0))
+        for item in todo:
+            grads_of(*item)
     now, own = 2 * (last % 2), 2 * ((last + 1) % 2)
-    pass_on(last, 0, 0, now)
-    pass_on(last, 1, 0, now + 1)
-    grads_of(0, own)
+    for part in range(PIECES // 2):
+        pass_on(last, 0, part, now)
+        pass_on(last, 1, part, now + 1)
+        for piece in range(work):
+            if piece * (PIECES // 2) // work == part:
+                grads_of(0, own, piece)
 
     @pl.loop(0, 2 * HEADS)
     def _(index):
@@ -493,8 +510,9 @@
 
     far = send(core_out.at[1], core_in.at[1], col_send.at[1], col_recv.at[1], core_peer)
     near = send(core_out.at[0], core_in.at[0], col_send.at[0], col_recv.at[0], core_peer)
-    pass_on(last, 0, 1, now)
-    pass_on(last, 1, 1, now + 1)
+    for part in range(PIECES // 2, PIECES):
+        pass_on(last, 0, part, now)
+        pass_on(last, 1, part, now + 1)
     far.wait_recv()
 
     @pl.loop(0, 2 * HEADS)
@@ -525,7 +543,7 @@
         saves.append(copy)
 
     for way in range(2):
-        for part in range(2):
+        for part in range(PIECES):
             sums[last, way, part].wait_recv()
     for k, ref in ((0, kgrad_ref), (1, vgrad_ref)):
         at = pl.ds(k * HEADS, HEADS)
@@ -576,10 +594,10 @@
             pltpu.VMEM((2 * HEADS, HEAD_DIM, wide), jnp.bfloat16),
             pltpu.VMEM((n_ring, HEADS, BLOCK, wide), jnp.float32),
             pltpu.VMEM((n_ring, HEADS, BLOCK, wide), jnp.float32),
-            pltpu.VMEM((n_ring, HEADS, 8, wide), jnp.float32),
-            pltpu.VMEM((4, HEADS, 8, wide), jnp.float32),
-            pltpu.VMEM((HEADS, n_ring, wide), jnp.float32),
-            pltpu.VMEM((HEADS, 8, wide), jnp.float32),
+            pltpu.VMEM((n_ring, 3, HEADS, wide), jnp.float32),
+            pltpu.VMEM((4, 3, HEADS, wide), jnp.float32),
+            pltpu.VMEM((n_ring, HEADS, wide), jnp.float32),
+            pltpu.VMEM((HEADS, wide), jnp.float32),
             pltpu.VMEM((2 * HEADS, HEAD_DIM, wide), jnp.float32),
             pltpu.VMEM((4,) + block, jnp.float32),
             pltpu.VMEM((half,) + block, jnp.bfloat16),
@@ -590,14 +608,14 @@
             pltpu.VMEM((2,) + block, jnp.bfloat16),
             pltpu.VMEM(block, jnp.bfloat16),
             pltpu.VMEM(block, jnp.bfloat16),
-            dma((4 * half,)),
-            dma((4 * half,)),
+            dma((2 * PIECES * half,)),
+            dma((2 * PIECES * half,)),
             dma((3,)),
             dma((3,)),
             dma((4,)),
             dma((4,)),
-            dma((4 * half,)),
-            dma((4 * half,)),
+            dma((2 * PIECES * half,)),
+            dma((2 * PIECES * half,)),
             dma((3,)),
             dma((3,)),
             dma((1,)),

time: 97 us -> 87.8 us (0.905)
  Pallas kernels: 95.5 us -> 86.4 us
    pallas_call x1, Pallas kernels: 93.4 us -> 84.2 us  [fused(): pl.pallas_call(functools.partial(layer_kernel, n_ring), out_shape=shapes,...]
where the time goes in v2:
time: 87.8 us; the launch traced here: 87.6 us
  Pallas kernels  86.4 us (98%)
  between operations  1.29 us (1%)
    pallas_call x1, Pallas kernels, fused(): pl.pallas_call(functools.partial(layer_kernel, n_ring), out_shape=shapes,...  84.2 us
    pallas_call x1, Pallas kernels, fused(): pl.pallas_call(write_kernel, out_shape=shapes, in_specs=[placed] * 4, out...  2.18 us

profile of v2, /device:TPU:0, one launch (start us, length us, event | category | flops | bytes accessed | tf_op | source)
XLA Modules:
  0.0 87.6 jit_solution(14397581810210547161)
XLA Ops:
  1.3 84.2 %shard_map.102 = (bf16[128,768]{1,0:T(8,128)(2,1)}, f32[128,768]{1,0:T(8,128)}, f32[128,768]{1,0:T(8,128)}, f32[128,768]{1,0:T(8,128)}) custom-call(s32[2,32]{1,0:T(2,128)} %bitcast.5, s32[1]{0:T(128)S(6)} %copy.11.count_ref, bf16[128,768]{1,0:T(8,128)(2,1)} %q_ref.1, bf16[128,768]{1,0:T(8,128)(2,1)} %k_ref.1, bf16[128,768]{1,0:T(8,128)(2,1)} %v_ref.1, ...), custom_call_target="tpu_custom_call" | custom-call | tf_op jit(solution)/shard_map/pallas_call | solution.py:581
  85.5 2.2 %shard_map.103 = (bf16[128,768]{1,0:T(8,128)(2,1)}, f32[128,768]{1,0:T(8,128)}, f32[128,768]{1,0:T(8,128)}, f32[128,768]{1,0:T(8,128)}) custom-call(bf16[128,768]{1,0:T(8,128)(2,1)} %get-tuple-element.8.refs_0_, f32[128,768]{1,0:T(8,128)} %get-tuple-element.9.refs_1_, f32[128,768]{1,0:T(8,128)} %get-tuple-element.10.refs_2_, ...), custom_call_target="tpu_custom_call" | custom-call | tf_op jit(solution)/shard_map/pallas_call | solution.py:629
